TPU v7x, 32 devices: a whole 2x2x4 slice. The times are simulated.
32 devices in a mesh: dp: 8 (over z, x), mp: 4 (over y, core).
Axes of the slice: x: 2, y: 2, z: 4, core: 2. Of those that a mesh axis runs over, the one named last changes fastest.
Arguments:
- preactivation: bfloat16 [3584, 32768], P('dp', 'mp'), may hold values from -6 to 6
- upstream: bfloat16 [3584, 512], P('dp'), may hold values from -0.29882812 to 0.29882812
- weight: bfloat16 [32768, 512], P('mp'), may hold values from -40 to 40
- first_moment: float32 [32768, 512], P(('mp', 'dp')), may hold values from -4 to 4
- second_moment: float32 [32768, 512], P(('mp', 'dp')), may hold values from 1 to 16
Outputs:
- input_grad: bfloat16 [3584, 32768], P('dp', 'mp')
- new_weight: bfloat16 [32768, 512], P('mp')
- first_next: float32 [32768, 512], P(('mp', 'dp'))
- second_next: float32 [32768, 512], P(('mp', 'dp'))
- trust_step: float32 [32768, 512], P(('mp', 'dp'))
All inputs are finite; a program needn't handle non-finite values.
Results may differ from a plain program's by a relative error of at most 0.015.
Values may be sent and summed in bfloat16 or wider, within the bound.
A program may use at most 128 MiB of HBM per device.

v0:
```python
import jax
import jax.numpy as jnp
from jax import lax
from jax.sharding import PartitionSpec as P

STEP = 1000


def per_device(preactivation, upstream, weight, first_moment, second_moment):
    owned = first_moment.shape[0]
    start_row = lax.axis_index("dp") * owned
    own_weight = lax.dynamic_slice_in_dim(weight, start_row, owned, 0).astype(jnp.float32)
    weight_local = jnp.sum(own_weight * own_weight)
    hidden = jnp.maximum(preactivation, jnp.zeros((), jnp.bfloat16))
    gradient = lax.psum_scatter(
        lax.dot_general(
            hidden, upstream, (((0,), (0,)), ((), ())), preferred_element_type=jnp.float32
        ).astype(jnp.bfloat16),
        "dp",
        scatter_dimension=0,
        tiled=True,
    ).astype(jnp.float32)
    back = lax.dot_general(
        upstream, weight, (((1,), (1,)), ((), ())), preferred_element_type=jnp.float32
    )
    input_grad = jnp.where(preactivation > 0, back, jnp.zeros((), jnp.float32)).astype(jnp.bfloat16)
    beta_one = 0.9
    beta_two = 0.999
    bias_one = 1.0 - beta_one**STEP
    bias_two = 1.0 - beta_two**STEP
    first_next = beta_one * first_moment + (1.0 - beta_one) * gradient
    second_next = beta_two * second_moment + (1.0 - beta_two) * gradient * gradient
    update = first_next / bias_one / (jnp.sqrt(second_next / bias_two) + 1e-06) + 0.02 * own_weight
    update_local = jnp.sum(update * update)
    weight_sq, update_sq = lax.psum((weight_local, update_local), ("dp", "mp"))
    trust_step = jnp.sqrt(weight_sq) / jnp.sqrt(update_sq) * update
    new_rows = (own_weight - 0.02 * trust_step).astype(jnp.bfloat16)
    new_weight = lax.all_gather(new_rows, "dp", axis=0, tiled=True)
    return (input_grad, new_weight, first_next, second_next, trust_step)


def solution(mesh):
    return jax.shard_map(
        per_device,
        mesh=mesh,
        in_specs=(
            P("dp", "mp"),
            P("dp", None),
            P("mp", None),
            P(("mp", "dp"), None),
            P(("mp", "dp"), None),
        ),
        out_specs=(
            P("dp", "mp"),
            P("mp", None),
            P(("mp", "dp"), None),
            P(("mp", "dp"), None),
            P(("mp", "dp"), None),
        ),
        check_vma=False,
    )
```

profile of v0, /device:TPU:0, one launch (start us, length us, event | category | flops | bytes accessed | tf_op | source)
XLA Modules:
  0.0 361.0 jit_solution(4923174628536832538)
XLA Ops:
  7.2 0.0 copy-start
  7.2 0.0 reduce-scatter.2.cloned.1.call-start
  7.2 1.0 copy-done
  8.2 10.1 %convolution_convert_fusion = bf16[8192,512]{1,0:T(8,128)(2,1)} fusion(bf16[448,512]{1,0:T(8,128)(2,1)S(1)} %copy-done, bf16[448,8192]{1,0:T(8,128)(2,1)} %param.5), kind=kOutput, calls=%fused_computation.1 | convolution fusion | flops 3765960704 | bytes 16187392 | tf_op jit(solution)/shard_map/dot_general | solution.py:16
  18.2 0.0 reduce-scatter.2.cloned.1.call-update
  18.3 0.0 all-gather.2.cloned.1.call-start
  18.3 152.2 %reduce-scatter.2.cloned.1.call-done = bf16[1024,512]{1,0:T(8,128)(2,1)} async-done(((bf16[8192,512]{1,0:T(8,128)(2,1)}), bf16[1024,512]{1,0:T(8,128)(2,1)}) %reduce-scatter.2.cloned.1.call-update) | async-done | bytes 1048592 | tf_op jit(solution)/shard_map/reduce_scatter | solution.py:15
  170.6 7.2 %multiply_reduce_fusion = (f32[]{:T(128)}, f32[1024,512]{1,0:T(8,128)S(1)}, f32[1024,512]{1,0:T(8,128)}, f32[1024,512]{1,0:T(8,128)}, f32[]{:T(128)}) fusion(bf16[8192,512]{1,0:T(8,128)(2,1)} %param.7, s32[]{:T(128)S(6)} %select_n.8, bf16[1024,512]{1,0:T(8,128)(2,1)} %reduce-scatter.2.cloned.1.call-done, f32[1024,512]{1,0:T(8,128)} %param.9, ...), kind=kLoop, calls=%fused_computation.14 | loop fusion | flops 9437182 | bytes 12582924 | tf_op jit(solution)/shard_map/reduce_sum | solution.py:34
  177.8 39.4 %all-reduce = (f32[]{:T(128)}, f32[]{:T(128)}) all-reduce(f32[]{:T(128)} %get-tuple-element.13, f32[]{:T(128)} %get-tuple-element.9), channel_id=1, replica_groups=mesh['dp'=8,'mp'=4] {'dp','mp'}, use_global_device_ids=true, to_apply=%region_1.0 | all-reduce | flops 2 | bytes 16 | tf_op jit(solution)/shard_map/psum | solution.py:35
  218.5 3.3 fusion.5
  221.8 0.0 all-gather.2.cloned.1.call-update
  221.9 11.7 %select_convert_fusion = bf16[448,8192]{1,0:T(8,128)(2,1)} fusion(bf16[448,8192]{1,0:T(8,128)(2,1)} %param.5, bf16[448,512]{1,0:T(8,128)(2,1)S(1)} %copy-done, bf16[8192,512]{1,0:T(8,128)(2,1)} %param.7), kind=kOutput, calls=%fused_computation | convolution fusion | flops 3769106432 | bytes 23527424 | tf_op jit(solution)/shard_map/dot_general | solution.py:23
  233.5 113.3 %all-gather.2.cloned.1.call-done = bf16[8192,512]{1,0:T(8,128)(2,1)} async-done(((bf16[1024,512]{1,0:T(8,128)(2,1)}), bf16[8192,512]{1,0:T(8,128)(2,1)}) %all-gather.2.cloned.1.call-update) | async-done | bytes 8388624 | tf_op jit(solution)/shard_map/all_gather | solution.py:38
  346.8 7.3 %copy.11 = bf16[8192,512]{1,0:T(8,128)(2,1)} copy(bf16[8192,512]{1,0:T(8,128)(2,1)} %all-gather.2.cloned.1.call-done) | data formatting | bytes 16777216
Async XLA Ops:
  7.2 1.0 copy-start
  7.2 163.4 %reduce-scatter.2.cloned.1.call-start = ((), (), s32[]{:S(2)}) async-start(), calls=%async_computation.1 | async-start | bytes 9437184 | tf_op jit(solution)/shard_map/reduce_scatter | solution.py:15
  18.3 328.6 %all-gather.2.cloned.1.call-start = ((), (), s32[]{:S(2)}) async-start(), calls=%async_computation.2 | async-start | bytes 9437184 | tf_op jit(solution)/shard_map/all_gather | solution.py:38
Sparse Core Ops, SparseCore 0:
  18.4 152.1 reduce-scatter.1
  222.0 124.8 all-gather.1
where the time goes:
time: 361 us
  waiting for transfers between devices  266 us (74%)
  blocking collectives  39.4 us (11%)
  matrix products  21.7 us (6%)
  between operations  15.4 us (4%)
  other arithmetic  10.5 us (3%)
  local copies, waits for them, and re-layouts  8.29 us (2%)
    reduce_scatter x1, waiting for transfers between devices, per_device(): lax.psum_scatter(lax.dot_general(hidden, upstream, (((0,), (0,)), ((), ()...  152 us
    all_gather x1, waiting for transfers between devices, per_device(): new_weight = lax.all_gather(new_rows, 'dp', axis=0, tiled=True)  113 us
    psum x1, blocking collectives, per_device(): weight_sq, update_sq = lax.psum((weight_local, update_local), ('dp', 'mp'))  39.4 us
    dot_general x1, matrix products, per_device(): lax.dot_general(upstream, weight, (((1,), (1,)), ((), ())), preferred_ele...  11.7 us
    dot_general x1, matrix products, per_device(): lax.dot_general(hidden, upstream, (((0,), (0,)), ((), ())), preferred_ele...  10.1 us
    unnamed x3, local copies, waits for them, and re-layouts  8.29 us
    reduce_sum x1, other arithmetic, per_device(): update_local = jnp.sum(update * update)  7.23 us
  transfers between devices with their start and end apart: 2, of which 2 were waited for; matrix products, arithmetic and copies ran while one was open for 3% of the time, Pallas kernels for 0%

commit v1 on v0

v1 whole, which is shorter than its diff:
```python
import functools

import jax
import jax.numpy as jnp
from jax import lax
from jax.experimental import pallas as pl
from jax.experimental.pallas import tpu as pltpu
from jax.sharding import PartitionSpec as P

STEP = 1000
BETA_ONE = 0.9
BETA_TWO = 0.999
BIAS_ONE = 1.0 - BETA_ONE**STEP
BIAS_TWO = 1.0 - BETA_TWO**STEP
MESH = pl.DeviceIdType.MESH


def moments(gradient, first_moment, second_moment, own_weight):
    first_next = BETA_ONE * first_moment + (1.0 - BETA_ONE) * gradient
    second_next = BETA_TWO * second_moment + (1.0 - BETA_TWO) * gradient * gradient
    update = first_next / BIAS_ONE / (jnp.sqrt(second_next / BIAS_TWO) + 1e-06) + 0.02 * own_weight
    return first_next, second_next, update


def kernel(
    nz, nmp, chunks, lag,
    pre, ups, w_hbm, m, v,
    g_out, upd, nrm,
    xs, xr, zb, ub, wv, acc, nsend, nrecv,
    xs_s, xr_s, zs_s, zr_s, ax_s, az_s, ar_s, own_s, w_s, ns_s, nr_s,
):
    dp = lax.axis_index("dp")
    mp = lax.axis_index("mp")
    z, x = dp // 2, dp % 2
    rows = m.shape[0]
    part = rows // chunks
    steps = nz * chunks
    partner = 2 * z + 1 - x
    below, above = dp - 2, dp + 2

    flips = []
    bit = 1
    while bit < 2 * nz:
        flips.append({"dp": dp + bit * (1 - 2 * ((dp // bit) % 2))})
        bit *= 2
    bit = 1
    while bit < nmp:
        flips.append({"mp": mp + bit * (1 - 2 * ((mp // bit) % 2))})
        bit *= 2

    w_copy = pltpu.make_async_copy(
        w_hbm.at[pl.ds(pl.multiple_of(dp * rows, rows), rows)], wv, w_s
    )
    w_copy.start()

    barrier = pltpu.get_barrier_semaphore()
    for k, device in enumerate(flips):
        if k != 1:
            pl.semaphore_signal(barrier, inc=1, device_id=device, device_id_type=MESH)

    @pl.when(z > 0)
    def _():
        pl.semaphore_signal(barrier, inc=1, device_id={"dp": below}, device_id_type=MESH)

    @pl.when(z < nz - 1)
    def _():
        pl.semaphore_signal(barrier, inc=1, device_id={"dp": above}, device_id_type=MESH)

    ends = jnp.where(z > 0, 1, 0) + jnp.where(z < nz - 1, 1, 0)
    pl.semaphore_wait(barrier, len(flips) - 1 + ends)

    def order(j):
        up, down = nz - 1 - z, z
        short = jnp.minimum(up, down)
        single = nz - 1 - 2 * short
        toward = jnp.where(up >= down, 1, -1)
        t = jnp.maximum(j - single, 0)
        dist = jnp.where(j < single, jnp.maximum(up, down) - j, short - t // 2)
        side = jnp.where(j < single, 1, 1 - 2 * (t % 2))
        return z + toward * side * dist

    def partial_of(dest, column, c):
        at = pl.multiple_of((2 * dest + column) * rows + c * part, part)
        hidden = jnp.maximum(pre[:, pl.ds(at, part)], jnp.zeros((), jnp.bfloat16))
        return lax.dot_general(
            hidden, ups[...], (((0,), (0,)), ((), ())), preferred_element_type=jnp.float32
        )

    def remote(src, dst, send, recv, device):
        return pltpu.make_async_remote_copy(
            src_ref=src, dst_ref=dst, send_sem=send, recv_sem=recv,
            device_id={"dp": device}, device_id_type=MESH,
        )

    def x_copy(k):
        return remote(xs.at[k], xr.at[k], xs_s.at[k], xr_s.at[k], partner)

    def z_copy(way, k, device):
        at = way * steps + k
        return remote(zb.at[at], zb.at[at], zs_s.at[at], zr_s.at[at], device)

    def shard_rows(shard, c):
        return pl.ds(pl.multiple_of(shard * rows + c * part, part), part)

    def own_rows(c):
        return pl.ds(pl.multiple_of(c * part, part), part)

    def ag_copy(src, place, c, send, device, column):
        at = shard_rows(2 * place + column, c)
        recv = ar_s.at[(2 * place + column) * chunks + c]
        return remote(src, upd.at[at], send, recv, device)

    def own_copy(c):
        return pltpu.make_async_copy(
            ub.at[own_rows(c)], upd.at[shard_rows(dp, c)], own_s.at[c]
        )

    def send_x(t, carry):
        c, dest = t // nz, order(t % nz)
        k = c * nz + dest
        xs[k] = partial_of(dest, 1 - x, c).astype(jnp.bfloat16)
        x_copy(k).start()
        return carry

    lax.fori_loop(0, steps, send_x, 0)
    w_copy.wait()
    acc[...] = jnp.zeros_like(acc)

    def rs_step(t):
        c, dest = t // nz, order(t % nz)
        k = c * nz + dest
        total = partial_of(dest, x, c)
        x_copy(k).wait_recv()
        total = total + xr[k].astype(jnp.float32)
        g_out[own_rows(c)] = total

        @pl.when((dest >= z) & (z > 0))
        def _():
            z_copy(0, k, below).wait_recv()
            g_out[own_rows(c)] += zb[k].astype(jnp.float32)

        @pl.when((dest <= z) & (z < nz - 1))
        def _():
            z_copy(1, k, above).wait_recv()
            g_out[own_rows(c)] += zb[steps + k].astype(jnp.float32)

        @pl.when(dest > z)
        def _():
            zb[k] = g_out[own_rows(c)].astype(jnp.bfloat16)
            z_copy(0, k, above).start()

        @pl.when(dest < z)
        def _():
            zb[steps + k] = g_out[own_rows(c)].astype(jnp.bfloat16)
            z_copy(1, k, below).start()

        @pl.when(dest == z)
        def _():
            own_weight = wv[own_rows(c)].astype(jnp.float32)
            _, _, update = moments(g_out[own_rows(c)], m[own_rows(c)], v[own_rows(c)], own_weight)
            ub[own_rows(c)] = update.astype(jnp.bfloat16)
            own_copy(c).start()
            acc[0:1] += jnp.sum(own_weight * own_weight, axis=0, keepdims=True)
            acc[1:2] += jnp.sum(update * update, axis=0, keepdims=True)

    def ag_sends(t, act):
        c, place = t // nz, order(nz - 1 - t % nz)
        k = c * nz + place

        @pl.when(place == z)
        def _():
            src = ub.at[own_rows(c)]

            @pl.when(z < nz - 1)
            def _():
                act(ag_copy(src, place, c, az_s.at[k], above, x))

            @pl.when(z > 0)
            def _():
                act(ag_copy(src, place, c, az_s.at[steps + k], below, x))

            act(ag_copy(src, place, c, ax_s.at[k], partner, x))

        @pl.when(place != z)
        def _():
            src = upd.at[shard_rows(2 * place + x, c)]

            @pl.when((place < z) & (z < nz - 1))
            def _():
                act(ag_copy(src, place, c, az_s.at[k], above, x))

            @pl.when((place > z) & (z > 0))
            def _():
                act(ag_copy(src, place, c, az_s.at[steps + k], below, x))

            act(ag_copy(src, place, c, ax_s.at[k], partner, x))

    def ag_step(t):
        c, place = t // nz, order(nz - 1 - t % nz)

        @pl.when(place != z)
        def _():
            src = upd.at[shard_rows(2 * place + x, c)]
            ag_copy(src, place, c, ax_s.at[0], partner, x).wait_recv()

        ag_sends(t, lambda copy: copy.start())

    def body(t, carry):
        rs_step(t)

        @pl.when(t >= lag)
        def _():
            ag_step(t - lag)

        return carry

    lax.fori_loop(0, steps, body, 0)

    width = acc.shape[1] // 128
    local = acc[:, 0:128]
    for q in range(1, width):
        local = local + acc[:, q * 128 : (q + 1) * 128]

    def norm_copy(k):
        return pltpu.make_async_remote_copy(
            src_ref=nsend.at[k], dst_ref=nrecv.at[k], send_sem=ns_s.at[k],
            recv_sem=nr_s.at[k], device_id=flips[k], device_id_type=MESH,
        )

    nsend[0] = local
    norm_copy(0).start()
    done = 0
    for t in range(lag):
        ag_step(steps - lag + t)
        while done < min(len(flips), (t + 1) * 2):
            norm_copy(done).wait()
            local = nsend[done] + nrecv[done]
            done += 1
            if done < len(flips):
                nsend[done] = local
                norm_copy(done).start()
    while done < len(flips):
        norm_copy(done).wait()
        local = nsend[done] + nrecv[done]
        done += 1
        if done < len(flips):
            nsend[done] = local
            norm_copy(done).start()
    nrm[...] = local

    def drain(t, carry):
        c, place = t // nz, t % nz
        k = c * nz + place
        x_copy(k).wait_send()

        @pl.when(place > z)
        def _():
            z_copy(0, k, above).wait_send()

        @pl.when(place < z)
        def _():
            z_copy(1, k, below).wait_send()

        ag_sends(t, lambda copy: copy.wait_send())
        src = upd.at[shard_rows(2 * place + 1 - x, c)]
        ag_copy(src, place, c, ax_s.at[0], partner, 1 - x).wait_recv()
        return carry

    lax.fori_loop(0, steps, drain, 0)
    for c in range(chunks):
        own_copy(c).wait()


def exchange(nz, nmp, preactivation, upstream, weight, first_moment, second_moment):
    rows, width = first_moment.shape
    part = min(rows, 256)
    chunks = rows // part
    steps = nz * chunks
    flips = (2 * nz).bit_length() - 1 + nmp.bit_length() - 1
    dma = pltpu.SemaphoreType.DMA
    vmem = pl.BlockSpec(memory_space=pltpu.VMEM)
    anyspec = pl.BlockSpec(memory_space=pl.ANY)
    return pl.pallas_call(
        functools.partial(kernel, nz, nmp, chunks, nz),
        out_shape=(
            jax.ShapeDtypeStruct((rows, width), jnp.float32),
            jax.ShapeDtypeStruct(weight.shape, jnp.bfloat16),
            jax.ShapeDtypeStruct((8, 128), jnp.float32),
        ),
        in_specs=[vmem, vmem, anyspec, vmem, vmem],
        out_specs=(vmem, anyspec, vmem),
        scratch_shapes=[
            pltpu.VMEM((steps, part, width), jnp.bfloat16),
            pltpu.VMEM((steps, part, width), jnp.bfloat16),
            pltpu.VMEM((2 * steps, part, width), jnp.bfloat16),
            pltpu.VMEM((rows, width), jnp.bfloat16),
            pltpu.VMEM((rows, width), jnp.bfloat16),
            pltpu.VMEM((8, width), jnp.float32),
            pltpu.VMEM((flips, 8, 128), jnp.float32),
            pltpu.VMEM((flips, 8, 128), jnp.float32),
            dma((steps,)),
            dma((steps,)),
            dma((2 * steps,)),
            dma((2 * steps,)),
            dma((steps,)),
            dma((2 * steps,)),
            dma((2 * steps,)),
            dma((chunks,)),
            dma,
            dma((flips,)),
            dma((flips,)),
        ],
        compiler_params=pltpu.CompilerParams(
            collective_id=0, has_side_effects=True, vmem_limit_bytes=56 * 2**20
        ),
    )(preactivation, upstream, weight, first_moment, second_moment)


def per_device(nz, nmp, preactivation, upstream, weight, first_moment, second_moment):
    owned = first_moment.shape[0]
    gradient, updates, norms = exchange(
        nz, nmp, preactivation, upstream, weight, first_moment, second_moment
    )
    back = lax.dot_general(
        upstream, weight, (((1,), (1,)), ((), ())), preferred_element_type=jnp.float32
    )
    input_grad = jnp.where(preactivation > 0, back, jnp.zeros((), jnp.float32)).astype(jnp.bfloat16)
    start_row = lax.axis_index("dp") * owned
    own_weight = lax.dynamic_slice_in_dim(weight, start_row, owned, 0).astype(jnp.float32)
    first_next, second_next, update = moments(gradient, first_moment, second_moment, own_weight)
    ratio = jnp.sqrt(jnp.sum(norms[0])) / jnp.sqrt(jnp.sum(norms[1]))
    trust_step = ratio * update
    new_weight = (
        weight.astype(jnp.float32) - 0.02 * (ratio * updates.astype(jnp.float32))
    ).astype(jnp.bfloat16)
    return (input_grad, new_weight, first_next, second_next, trust_step)


def solution(mesh):
    return jax.shard_map(
        functools.partial(per_device, mesh.shape["dp"] // 2, mesh.shape["mp"]),
        mesh=mesh,
        in_specs=(
            P("dp", "mp"),
            P("dp", None),
            P("mp", None),
            P(("mp", "dp"), None),
            P(("mp", "dp"), None),
        ),
        out_specs=(
            P("dp", "mp"),
            P("mp", None),
            P(("mp", "dp"), None),
            P(("mp", "dp"), None),
            P(("mp", "dp"), None),
        ),
        check_vma=False,
    )
```

time: 361 us -> 230 us (0.64)
  waiting for transfers between devices: 266 us -> 0 us
  Pallas kernels: 0 us -> 200 us
  blocking collectives: 39.4 us -> 0 us
  between operations: 15.4 us -> 2.05 us
  matrix products: 21.7 us -> 11.6 us
  local copies, waits for them, and re-layouts: 8.29 us -> 0.01 us
  other arithmetic: 10.5 us -> 16.2 us
    pallas_call x0 -> x1, Pallas kernels: none -> 200 us  [exchange(): pl.pallas_call(functools.partial(kernel, nz, nmp, chunks, nz), out_shape=...]
    reduce_scatter x1 -> x0, waiting for transfers between devices: 152 us -> none  [per_device(): lax.psum_scatter(lax.dot_general(hidden, upstream, (((0,), (0,)), ((), ()...]
    all_gather x1 -> x0, waiting for transfers between devices: 113 us -> none  [per_device(): new_weight = lax.all_gather(new_rows, 'dp', axis=0, tiled=True)]
    psum x1 -> x0, blocking collectives: 39.4 us -> none  [per_device(): weight_sq, update_sq = lax.psum((weight_local, update_local), ('dp', 'mp'))]
    dot_general x1 -> x0, matrix products: 10.1 us -> none  [per_device(): lax.dot_general(hidden, upstream, (((0,), (0,)), ((), ())), preferred_ele...]
    unnamed x3 -> x6, local copies, waits for them, and re-layouts: 8.29 us -> 0.01 us
    mul x0 -> x1, other arithmetic: none -> 6.47 us  [per_device(): trust_step = ratio * update]
    reduce_sum x1, other arithmetic: 7.23 us -> 1.37 us  [per_device(): ratio = jnp.sqrt(jnp.sum(norms[0])) / jnp.sqrt(jnp.sum(norms[1]))]
  transfers between devices with their start and end apart: 2 -> 0, of which waited for: 2 -> 0; matrix products, arithmetic and copies ran while one was open for 3% -> 0% of each run, Pallas kernels for 0% -> 0%
where the time goes in v1:
time: 230 us
  Pallas kernels  200 us (87%)
  other arithmetic  16.2 us (7%)
  matrix products  11.6 us (5%)
    pallas_call x1, Pallas kernels, exchange(): pl.pallas_call(functools.partial(kernel, nz, nmp, chunks, nz), out_shape=...  200 us
    dot_general x1, matrix products, per_device(): lax.dot_general(upstream, weight, (((1,), (1,)), ((), ())), preferred_ele...  11.6 us
    convert_element_type x1, other arithmetic, per_device(): new_weight = (weight.astype(jnp.float32) - 0.02 * (ratio * updates.astype...  8.4 us
    mul x1, other arithmetic, per_device(): trust_step = ratio * update  6.47 us

profile of v1, /device:TPU:0, one launch (start us, length us, event | category | flops | bytes accessed | tf_op | source)
XLA Modules:
  0.0 230.0 jit_solution(10556335427945095103)
XLA Ops:
  0.6 0.0 copy-start.1
  0.6 200.0 %shard_map.92 = (f32[1024,512]{1,0:T(8,128)}, bf16[8192,512]{1,0:T(8,128)(2,1)}, f32[8,128]{1,0:T(8,128)}) custom-call(bf16[448,8192]{1,0:T(8,128)(2,1)} %pre.1, bf16[448,512]{1,0:T(8,128)(2,1)} %ups.1, bf16[8192,512]{1,0:T(8,128)(2,1)} %w_hbm.1, f32[1024,512]{1,0:T(8,128)} %m.1, f32[1024,512]{1,0:T(8,128)} %v.1), custom_call_target="tpu_custom_call" | custom-call | tf_op jit(solution)/shard_map/pallas_call | solution.py:283
  200.7 1.4 slice_reduce_fusion
  203.4 0.0 copy-done.1
  203.4 0.0 copy-start
  203.5 6.5 %add_multiply_fusion = (f32[1024,512]{1,0:T(8,128)}, f32[1024,512]{1,0:T(8,128)}, f32[1024,512]{1,0:T(8,128)}) fusion(bf16[8192,512]{1,0:T(8,128)(2,1)} %w_hbm.1, s32[]{:T(128)S(6)} %select_n.8, f32[]{:T(128)S(6)} %div.14, f32[1024,512]{1,0:T(8,128)} %get-tuple-element.10, f32[1024,512]{1,0:T(8,128)} %v.1, f32[1024,512]{1,0:T(8,128)S(1)} %copy-done.1), kind=kLoop, calls=%fused_computation.4 | loop fusion | flops 7340032 | bytes 13631496 | tf_op jit(solution)/shard_map/mul | solution.py:332
  209.9 0.0 copy-done
  209.9 0.0 copy-start.2
  209.9 8.4 %subtract_convert_fusion = bf16[8192,512]{1,0:T(8,128)(2,1)} fusion(bf16[8192,512]{1,0:T(8,128)(2,1)} %get-tuple-element.9, bf16[8192,512]{1,0:T(8,128)(2,1)S(1)} %copy-done, f32[]{:T(128)S(6)} %div.14), kind=kLoop, calls=%fused_computation | loop fusion | flops 25165824 | bytes 25165828 | tf_op jit(solution)/shard_map/convert_element_type | solution.py:335
  218.3 0.0 copy-done.2
  218.3 11.6 %select_convert_fusion = bf16[448,8192]{1,0:T(8,128)(2,1)} fusion(bf16[448,8192]{1,0:T(8,128)(2,1)} %pre.1, bf16[448,512]{1,0:T(8,128)(2,1)S(1)} %copy-done.2, bf16[8192,512]{1,0:T(8,128)(2,1)} %w_hbm.1), kind=kOutput, calls=%fused_computation.1 | convolution fusion | flops 3769106432 | bytes 23527424 | tf_op jit(solution)/shard_map/dot_general | solution.py:324
Async XLA Ops:
  0.6 202.8 %copy-start.1 = (f32[1024,512]{1,0:T(8,128)S(1)}, f32[1024,512]{1,0:T(8,128)}, u32[]{:S(2)}) copy-start(f32[1024,512]{1,0:T(8,128)} %m.1) | copy-start | bytes 6291460
  203.4 6.5 %copy-start = (bf16[8192,512]{1,0:T(8,128)(2,1)S(1)}, bf16[8192,512]{1,0:T(8,128)(2,1)}, u32[]{:S(2)}) copy-start(bf16[8192,512]{1,0:T(8,128)(2,1)} %w_hbm.1) | copy-start | bytes 25165828
  209.9 8.4 %copy-start.2 = (bf16[448,512]{1,0:T(8,128)(2,1)S(1)}, bf16[448,512]{1,0:T(8,128)(2,1)}, u32[]{:S(2)}) copy-start(bf16[448,512]{1,0:T(8,128)(2,1)} %ups.1) | copy-start | bytes 1376260

commit v2 on v1

--- a/solution.py
+++ b/solution.py
@@ -23,20 +23,23 @@
 
 
 def kernel(
-    nz, nmp, chunks, lag,
+    nz, nmp, chunks, first_rows, lead,
     pre, ups, w_hbm, m, v,
     g_out, upd, nrm,
-    xs, xr, zb, ub, wv, acc, nsend, nrecv,
-    xs_s, xr_s, zs_s, zr_s, ax_s, az_s, ar_s, own_s, w_s, ns_s, nr_s,
+    xs, xr, qs, qxs, qxr, zb, tb, ub, wv, acc, nsend, nrecv,
+    xs_s, xr_s, qs_s, qr_s, zs_s, zr_s, ax_s, az_s, aqx_s, aqz_s,
+    arz_s, arx_s, arq_s, own_s, w_s, ns_s, nr_s,
 ):
     dp = lax.axis_index("dp")
     mp = lax.axis_index("mp")
     z, x = dp // 2, dp % 2
     rows = m.shape[0]
     part = rows // chunks
+    rest = part - first_rows
     steps = nz * chunks
     partner = 2 * z + 1 - x
     below, above = dp - 2, dp + 2
+    lag = nz + 1
 
     flips = []
     bit = 1
@@ -95,126 +98,179 @@
     def x_copy(k):
         return remote(xs.at[k], xr.at[k], xs_s.at[k], xr_s.at[k], partner)
 
+    def q_copy(c):
+        return remote(qxs.at[c], qxr.at[c], qs_s.at[c], qr_s.at[c], partner)
+
     def z_copy(way, k, device):
         at = way * steps + k
         return remote(zb.at[at], zb.at[at], zs_s.at[at], zr_s.at[at], device)
 
-    def shard_rows(shard, c):
-        return pl.ds(pl.multiple_of(shard * rows + c * part, part), part)
-
     def own_rows(c):
         return pl.ds(pl.multiple_of(c * part, part), part)
 
-    def ag_copy(src, place, c, send, device, column):
-        at = shard_rows(2 * place + column, c)
-        recv = ar_s.at[(2 * place + column) * chunks + c]
-        return remote(src, upd.at[at], send, recv, device)
+    def own_first(c):
+        return pl.ds(pl.multiple_of(c * part, part), first_rows)
+
+    def own_rest(c):
+        return pl.ds(pl.multiple_of(c * part + first_rows, 16), rest)
+
+    def all_of(shard, c):
+        return upd.at[pl.ds(pl.multiple_of(shard * rows + c * part, part), part)]
+
+    def first_of(shard, c):
+        return upd.at[pl.ds(pl.multiple_of(shard * rows + c * part, part), first_rows)]
+
+    def rest_of(shard, c):
+        return upd.at[pl.ds(pl.multiple_of(shard * rows + c * part + first_rows, 16), rest)]
 
     def own_copy(c):
-        return pltpu.make_async_copy(
-            ub.at[own_rows(c)], upd.at[shard_rows(dp, c)], own_s.at[c]
-        )
-
-    def send_x(t, carry):
+        return pltpu.make_async_copy(ub.at[own_rows(c)], all_of(dp, c), own_s.at[c])
+
+    def send_x(t):
         c, dest = t // nz, order(t % nz)
         k = c * nz + dest
-        xs[k] = partial_of(dest, 1 - x, c).astype(jnp.bfloat16)
+        total = partial_of(dest, 1 - x, c)
+        xs[k] = total[:first_rows].astype(jnp.bfloat16)
+        qs[k] = total[first_rows:].astype(jnp.bfloat16)
         x_copy(k).start()
-        return carry
-
-    lax.fori_loop(0, steps, send_x, 0)
-    w_copy.wait()
-    acc[...] = jnp.zeros_like(acc)
 
     def rs_step(t):
         c, dest = t // nz, order(t % nz)
         k = c * nz + dest
-        total = partial_of(dest, x, c)
+        tb[0:part] = partial_of(dest, x, c)
+        tb[part:] = qs[k].astype(jnp.float32)
         x_copy(k).wait_recv()
-        total = total + xr[k].astype(jnp.float32)
-        g_out[own_rows(c)] = total
+        tb[0:first_rows] += xr[k].astype(jnp.float32)
 
         @pl.when((dest >= z) & (z > 0))
         def _():
             z_copy(0, k, below).wait_recv()
-            g_out[own_rows(c)] += zb[k].astype(jnp.float32)
+            tb[...] += zb[k].astype(jnp.float32)
 
         @pl.when((dest <= z) & (z < nz - 1))
         def _():
             z_copy(1, k, above).wait_recv()
-            g_out[own_rows(c)] += zb[steps + k].astype(jnp.float32)
+            tb[...] += zb[steps + k].astype(jnp.float32)
 
         @pl.when(dest > z)
         def _():
-            zb[k] = g_out[own_rows(c)].astype(jnp.bfloat16)
+            zb[k] = tb[...].astype(jnp.bfloat16)
             z_copy(0, k, above).start()
 
         @pl.when(dest < z)
         def _():
-            zb[steps + k] = g_out[own_rows(c)].astype(jnp.bfloat16)
+            zb[steps + k] = tb[...].astype(jnp.bfloat16)
             z_copy(1, k, below).start()
 
         @pl.when(dest == z)
         def _():
-            own_weight = wv[own_rows(c)].astype(jnp.float32)
-            _, _, update = moments(g_out[own_rows(c)], m[own_rows(c)], v[own_rows(c)], own_weight)
-            ub[own_rows(c)] = update.astype(jnp.bfloat16)
-            own_copy(c).start()
-            acc[0:1] += jnp.sum(own_weight * own_weight, axis=0, keepdims=True)
-            acc[1:2] += jnp.sum(update * update, axis=0, keepdims=True)
+            g_out[own_rows(c)] = tb[0:part]
+            qxs[c] = tb[part:].astype(jnp.bfloat16)
+            q_copy(c).start()
+
+    def finish(c):
+        q_copy(c).wait_recv()
+        g_out[own_rest(c)] += qxr[c].astype(jnp.float32)
+        own_weight = wv[own_rows(c)].astype(jnp.float32)
+        _, _, update = moments(g_out[own_rows(c)], m[own_rows(c)], v[own_rows(c)], own_weight)
+        ub[own_rows(c)] = update.astype(jnp.bfloat16)
+        own_copy(c).start()
+        acc[0:1] += jnp.sum(own_weight * own_weight, axis=0, keepdims=True)
+        acc[1:2] += jnp.sum(update * update, axis=0, keepdims=True)
 
     def ag_sends(t, act):
         c, place = t // nz, order(nz - 1 - t % nz)
         k = c * nz + place
+        shard = 2 * place + x
+
+        def sends(whole, first):
+            @pl.when((place <= z) & (z < nz - 1))
+            def _():
+                act(remote(whole, all_of(shard, c), az_s.at[k], arz_s.at[k], above))
+
+            @pl.when((place >= z) & (z > 0))
+            def _():
+                at = steps + k
+                act(remote(whole, all_of(shard, c), az_s.at[at], arz_s.at[k], below))
+
+            act(remote(first, first_of(shard, c), ax_s.at[k], arx_s.at[k], partner))
 
         @pl.when(place == z)
         def _():
-            src = ub.at[own_rows(c)]
-
-            @pl.when(z < nz - 1)
-            def _():
-                act(ag_copy(src, place, c, az_s.at[k], above, x))
-
-            @pl.when(z > 0)
-            def _():
-                act(ag_copy(src, place, c, az_s.at[steps + k], below, x))
-
-            act(ag_copy(src, place, c, ax_s.at[k], partner, x))
+            act(
+                remote(
+                    ub.at[own_rest(c)], rest_of(shard, c), aqx_s.at[c], arq_s.at[k], partner
+                )
+            )
+            sends(ub.at[own_rows(c)], ub.at[own_first(c)])
 
         @pl.when(place != z)
         def _():
-            src = upd.at[shard_rows(2 * place + x, c)]
-
-            @pl.when((place < z) & (z < nz - 1))
-            def _():
-                act(ag_copy(src, place, c, az_s.at[k], above, x))
-
-            @pl.when((place > z) & (z > 0))
-            def _():
-                act(ag_copy(src, place, c, az_s.at[steps + k], below, x))
-
-            act(ag_copy(src, place, c, ax_s.at[k], partner, x))
+            sends(all_of(shard, c), first_of(shard, c))
+
+    def agq_sends(t, act):
+        c, place = t // nz, order(nz - 1 - t % nz)
+        k = c * nz + place
+        block = rest_of(2 * place + 1 - x, c)
+
+        @pl.when((place <= z) & (z < nz - 1))
+        def _():
+            act(remote(block, block, aqz_s.at[k], arq_s.at[k], above))
+
+        @pl.when((place >= z) & (z > 0))
+        def _():
+            act(remote(block, block, aqz_s.at[steps + k], arq_s.at[k], below))
 
     def ag_step(t):
         c, place = t // nz, order(nz - 1 - t % nz)
+        k = c * nz + place
 
         @pl.when(place != z)
         def _():
-            src = upd.at[shard_rows(2 * place + x, c)]
-            ag_copy(src, place, c, ax_s.at[0], partner, x).wait_recv()
+            block = all_of(2 * place + x, c)
+            remote(block, block, az_s.at[k], arz_s.at[k], partner).wait_recv()
 
         ag_sends(t, lambda copy: copy.start())
 
+    def agq_step(t):
+        c, place = t // nz, order(nz - 1 - t % nz)
+        k = c * nz + place
+        block = rest_of(2 * place + 1 - x, c)
+        remote(block, block, aqz_s.at[k], arq_s.at[k], partner).wait_recv()
+        agq_sends(t, lambda copy: copy.start())
+
+    def start_x(t, carry):
+        send_x(t)
+        return carry
+
+    lax.fori_loop(0, lead, start_x, 0)
+    w_copy.wait()
+    acc[...] = jnp.zeros_like(acc)
+
     def body(t, carry):
-        rs_step(t)
+        @pl.when(t + lead < steps)
+        def _():
+            send_x(t + lead)
+
+        @pl.when(t < steps)
+        def _():
+            rs_step(t)
+
+        @pl.when((t >= nz) & (t % nz == 1))
+        def _():
+            finish(t // nz - 1)
 
         @pl.when(t >= lag)
         def _():
             ag_step(t - lag)
 
+        @pl.when(t >= lag + 1)
+        def _():
+            agq_step(t - lag - 1)
+
         return carry
 
-    lax.fori_loop(0, steps, body, 0)
+    lax.fori_loop(0, steps + 2, body, 0)
 
     width = acc.shape[1] // 128
     local = acc[:, 0:128]
@@ -230,22 +286,18 @@
     nsend[0] = local
     norm_copy(0).start()
     done = 0
-    for t in range(lag):
-        ag_step(steps - lag + t)
-        while done < min(len(flips), (t + 1) * 2):
-            norm_copy(done).wait()
-            local = nsend[done] + nrecv[done]
-            done += 1
+    for t in range(steps + 2, steps + lag + 1):
+        if t - lag < steps:
+            ag_step(t - lag)
+        agq_step(t - lag - 1)
+        for _ in range(2):
             if done < len(flips):
-                nsend[done] = local
-                norm_copy(done).start()
-    while done < len(flips):
-        norm_copy(done).wait()
-        local = nsend[done] + nrecv[done]
-        done += 1
-        if done < len(flips):
-            nsend[done] = local
-            norm_copy(done).start()
+                norm_copy(done).wait()
+                local = nsend[done] + nrecv[done]
+                done += 1
+                if done < len(flips):
+                    nsend[done] = local
+                    norm_copy(done).start()
     nrm[...] = local
 
     def drain(t, carry):
@@ -262,18 +314,22 @@
             z_copy(1, k, below).wait_send()
 
         ag_sends(t, lambda copy: copy.wait_send())
-        src = upd.at[shard_rows(2 * place + 1 - x, c)]
-        ag_copy(src, place, c, ax_s.at[0], partner, 1 - x).wait_recv()
+        agq_sends(t, lambda copy: copy.wait_send())
+        block = first_of(2 * place + 1 - x, c)
+        remote(block, block, ax_s.at[k], arx_s.at[k], partner).wait_recv()
         return carry
 
     lax.fori_loop(0, steps, drain, 0)
     for c in range(chunks):
         own_copy(c).wait()
+        q_copy(c).wait_send()
 
 
 def exchange(nz, nmp, preactivation, upstream, weight, first_moment, second_moment):
     rows, width = first_moment.shape
     part = min(rows, 256)
+    first_rows = part * 5 // 8
+    rest = part - first_rows
     chunks = rows // part
     steps = nz * chunks
     flips = (2 * nz).bit_length() - 1 + nmp.bit_length() - 1
@@ -281,7 +337,7 @@
     vmem = pl.BlockSpec(memory_space=pltpu.VMEM)
     anyspec = pl.BlockSpec(memory_space=pl.ANY)
     return pl.pallas_call(
-        functools.partial(kernel, nz, nmp, chunks, nz),
+        functools.partial(kernel, nz, nmp, chunks, first_rows, min(nz + 2, steps)),
         out_shape=(
             jax.ShapeDtypeStruct((rows, width), jnp.float32),
             jax.ShapeDtypeStruct(weight.shape, jnp.bfloat16),
@@ -290,9 +346,13 @@
         in_specs=[vmem, vmem, anyspec, vmem, vmem],
         out_specs=(vmem, anyspec, vmem),
         scratch_shapes=[
-            pltpu.VMEM((steps, part, width), jnp.bfloat16),
-            pltpu.VMEM((steps, part, width), jnp.bfloat16),
-            pltpu.VMEM((2 * steps, part, width), jnp.bfloat16),
+            pltpu.VMEM((steps, first_rows, width), jnp.bfloat16),
+            pltpu.VMEM((steps, first_rows, width), jnp.bfloat16),
+            pltpu.VMEM((steps, rest, width), jnp.bfloat16),
+            pltpu.VMEM((chunks, rest, width), jnp.bfloat16),
+            pltpu.VMEM((chunks, rest, width), jnp.bfloat16),
+            pltpu.VMEM((2 * steps, part + rest, width), jnp.bfloat16),
+            pltpu.VMEM((part + rest, width), jnp.float32),
             pltpu.VMEM((rows, width), jnp.bfloat16),
             pltpu.VMEM((rows, width), jnp.bfloat16),
             pltpu.VMEM((8, width), jnp.float32),
@@ -300,11 +360,17 @@
             pltpu.VMEM((flips, 8, 128), jnp.float32),
             dma((steps,)),
             dma((steps,)),
+            dma((chunks,)),
+            dma((chunks,)),
             dma((2 * steps,)),
             dma((2 * steps,)),
             dma((steps,)),
             dma((2 * steps,)),
+            dma((chunks,)),
             dma((2 * steps,)),
+            dma((steps,)),
+            dma((steps,)),
+            dma((steps,)),
             dma((chunks,)),
             dma,
             dma((flips,)),

time: 230 us -> 231 us (level)
  no operation moved by 1% of the time
where the time goes in v2:
time: 231 us
  Pallas kernels  201 us (87%)
  other arithmetic  16.2 us (7%)
  matrix products  11.7 us (5%)
    pallas_call x1, Pallas kernels, exchange(): pl.pallas_call(functools.partial(kernel, nz, nmp, chunks, first_rows, min...  201 us
    dot_general x1, matrix products, per_device(): lax.dot_general(upstream, weight, (((1,), (1,)), ((), ())), preferred_ele...  11.7 us
    convert_element_type x1, other arithmetic, per_device(): new_weight = (weight.astype(jnp.float32) - 0.02 * (ratio * updates.astype...  8.4 us
    mul x1, other arithmetic, per_device(): trust_step = ratio * update  6.47 us

profile of v2, /device:TPU:0, one launch (start us, length us, event | category | flops | bytes accessed | tf_op | source)
XLA Modules:
  0.0 230.9 jit_solution(12575099059935098198)
XLA Ops:
  0.6 0.0 copy-start.1
  0.6 200.9 %shard_map.92 = (f32[1024,512]{1,0:T(8,128)}, bf16[8192,512]{1,0:T(8,128)(2,1)}, f32[8,128]{1,0:T(8,128)}) custom-call(bf16[448,8192]{1,0:T(8,128)(2,1)} %pre.1, bf16[448,512]{1,0:T(8,128)(2,1)} %ups.1, bf16[8192,512]{1,0:T(8,128)(2,1)} %w_hbm.1, f32[1024,512]{1,0:T(8,128)} %m.1, f32[1024,512]{1,0:T(8,128)} %v.1), custom_call_target="tpu_custom_call" | custom-call | tf_op jit(solution)/shard_map/pallas_call | solution.py:339
  201.5 1.4 slice_reduce_fusion
  204.3 0.0 copy-done.1
  204.3 0.0 copy-start
  204.3 6.5 %add_multiply_fusion = (f32[1024,512]{1,0:T(8,128)}, f32[1024,512]{1,0:T(8,128)}, f32[1024,512]{1,0:T(8,128)}) fusion(bf16[8192,512]{1,0:T(8,128)(2,1)} %w_hbm.1, s32[]{:T(128)S(6)} %select_n.8, f32[]{:T(128)S(6)} %div.14, f32[1024,512]{1,0:T(8,128)} %get-tuple-element.10, f32[1024,512]{1,0:T(8,128)} %v.1, f32[1024,512]{1,0:T(8,128)S(1)} %copy-done.1), kind=kLoop, calls=%fused_computation.4 | loop fusion | flops 7340032 | bytes 13631496 | tf_op jit(solution)/shard_map/mul | solution.py:398
  210.8 0.0 copy-done
  210.8 0.0 copy-start.2
  210.8 8.4 %subtract_convert_fusion = bf16[8192,512]{1,0:T(8,128)(2,1)} fusion(bf16[8192,512]{1,0:T(8,128)(2,1)} %get-tuple-element.9, bf16[8192,512]{1,0:T(8,128)(2,1)S(1)} %copy-done, f32[]{:T(128)S(6)} %div.14), kind=kLoop, calls=%fused_computation | loop fusion | flops 25165824 | bytes 25165828 | tf_op jit(solution)/shard_map/convert_element_type | solution.py:401
  219.2 0.0 copy-done.2
  219.2 11.7 %select_convert_fusion = bf16[448,8192]{1,0:T(8,128)(2,1)} fusion(bf16[448,8192]{1,0:T(8,128)(2,1)} %pre.1, bf16[448,512]{1,0:T(8,128)(2,1)S(1)} %copy-done.2, bf16[8192,512]{1,0:T(8,128)(2,1)} %w_hbm.1), kind=kOutput, calls=%fused_computation.1 | convolution fusion | flops 3769106432 | bytes 23527424 | tf_op jit(solution)/shard_map/dot_general | solution.py:390
Async XLA Ops:
  0.6 203.7 %copy-start.1 = (f32[1024,512]{1,0:T(8,128)S(1)}, f32[1024,512]{1,0:T(8,128)}, u32[]{:S(2)}) copy-start(f32[1024,512]{1,0:T(8,128)} %m.1) | copy-start | bytes 6291460
  204.3 6.5 %copy-start = (bf16[8192,512]{1,0:T(8,128)(2,1)S(1)}, bf16[8192,512]{1,0:T(8,128)(2,1)}, u32[]{:S(2)}) copy-start(bf16[8192,512]{1,0:T(8,128)(2,1)} %w_hbm.1) | copy-start | bytes 25165828
  210.8 8.4 %copy-start.2 = (bf16[448,512]{1,0:T(8,128)(2,1)S(1)}, bf16[448,512]{1,0:T(8,128)(2,1)}, u32[]{:S(2)}) copy-start(bf16[448,512]{1,0:T(8,128)(2,1)} %ups.1) | copy-start | bytes 1376260

commit v3 on v2

--- a/solution.py
+++ b/solution.py
@@ -39,7 +39,7 @@
     steps = nz * chunks
     partner = 2 * z + 1 - x
     below, above = dp - 2, dp + 2
-    lag = nz + 1
+    lag = 2 * nz + 1
 
     flips = []
     bit = 1
@@ -247,58 +247,66 @@
     w_copy.wait()
     acc[...] = jnp.zeros_like(acc)
 
-    def body(t, carry):
-        @pl.when(t + lead < steps)
-        def _():
-            send_x(t + lead)
-
-        @pl.when(t < steps)
-        def _():
-            rs_step(t)
-
-        @pl.when((t >= nz) & (t % nz == 1))
-        def _():
-            finish(t // nz - 1)
-
-        @pl.when(t >= lag)
-        def _():
-            ag_step(t - lag)
-
-        @pl.when(t >= lag + 1)
-        def _():
-            agq_step(t - lag - 1)
-
-        return carry
-
-    lax.fori_loop(0, steps + 2, body, 0)
-
-    width = acc.shape[1] // 128
-    local = acc[:, 0:128]
-    for q in range(1, width):
-        local = local + acc[:, q * 128 : (q + 1) * 128]
-
     def norm_copy(k):
         return pltpu.make_async_remote_copy(
             src_ref=nsend.at[k], dst_ref=nrecv.at[k], send_sem=ns_s.at[k],
             recv_sem=nr_s.at[k], device_id=flips[k], device_id_type=MESH,
         )
 
-    nsend[0] = local
-    norm_copy(0).start()
-    done = 0
-    for t in range(steps + 2, steps + lag + 1):
-        if t - lag < steps:
-            ag_step(t - lag)
-        agq_step(t - lag - 1)
-        for _ in range(2):
-            if done < len(flips):
-                norm_copy(done).wait()
-                local = nsend[done] + nrecv[done]
-                done += 1
-                if done < len(flips):
-                    nsend[done] = local
-                    norm_copy(done).start()
-    nrm[...] = local
+    def norm_step(k):
+        if k == 0:
+            local = acc[:, 0:128]
+            for q in range(1, acc.shape[1] // 128):
+                local = local + acc[:, q * 128 : (q + 1) * 128]
+        else:
+            norm_copy(k - 1).wait()
+            local = nsend[k - 1] + nrecv[k - 1]
+        if k < len(flips):
+            nsend[k] = local
+            norm_copy(k).start()
+        else:
+            nrm[...] = local
+
+    last = steps + nz * ((nz - 1) // 2)
+    norm_at = steps + nz + 2
+
+    def late(u, act):
+        j = u % nz
+        c = u // nz - j // 2
+
+        @pl.when((u >= 0) & (c >= 0) & (c < chunks))
+        def _():
+            act(c * nz + j)
+
+    def body(t, carry):
+        @pl.when(t + lead < steps)
+        def _():
+            send_x(t + lead)
+
+        @pl.when((t < steps) & (t % nz != nz - 1))
+        def _():
+            rs_step(t)
+
+        @pl.when((t >= nz) & (t < steps + nz) & (t % nz == nz - 1))
+        def _():
+            rs_step(t - nz)
+
+        @pl.when((t >= 2 * nz) & (t < steps + 2 * nz) & (t % nz == 1))
+        def _():
+            finish(t // nz - 2)
+
+        late(t - lag, ag_step)
+        late(t - lag - 2, agq_step)
+        for k in range(len(flips)):
+
+            @pl.when(t == norm_at + k)
+            def _():
+                norm_step(k)
+
+        return carry
+
+    lax.fori_loop(0, last + lag + 2, body, 0)
+    norm_step(len(flips))
 
     def drain(t, carry):
         c, place = t // nz, t % nz
@@ -327,7 +335,7 @@
 
 def exchange(nz, nmp, preactivation, upstream, weight, first_moment, second_moment):
     rows, width = first_moment.shape
-    part = min(rows, 256)
+    part = min(rows, 128)
     first_rows = part * 5 // 8
     rest = part - first_rows
     chunks = rows // part
@@ -337,7 +345,7 @@
     vmem = pl.BlockSpec(memory_space=pltpu.VMEM)
     anyspec = pl.BlockSpec(memory_space=pl.ANY)
     return pl.pallas_call(
-        functools.partial(kernel, nz, nmp, chunks, first_rows, min(nz + 2, steps)),
+        functools.partial(kernel, nz, nmp, chunks, first_rows, min(2 * nz, steps)),
         out_shape=(
             jax.ShapeDtypeStruct((rows, width), jnp.float32),
             jax.ShapeDtypeStruct(weight.shape, jnp.bfloat16),

time: 231 us -> 267 us (1.16)
  Pallas kernels: 201 us -> 236 us
    pallas_call x1, Pallas kernels: 201 us -> 236 us  [exchange(): pl.pallas_call(functools.partial(kernel, nz, nmp, chunks, first_rows, min...]
where the time goes in v3:
time: 267 us; the launch traced here: 266 us
  Pallas kernels  236 us (88%)
  other arithmetic  16.2 us (6%)
  matrix products  11.6 us (4%)
    pallas_call x1, Pallas kernels, exchange(): pl.pallas_call(functools.partial(kernel, nz, nmp, chunks, first_rows, min...  236 us
    dot_general x1, matrix products, per_device(): lax.dot_general(upstream, weight, (((1,), (1,)), ((), ())), preferred_ele...  11.6 us
    convert_element_type x1, other arithmetic, per_device(): new_weight = (weight.astype(jnp.float32) - 0.02 * (ratio * updates.astype...  8.4 us
    mul x1, other arithmetic, per_device(): trust_step = ratio * update  6.47 us

profile of v3, /device:TPU:0, one launch (start us, length us, event | category | flops | bytes accessed | tf_op | source)
XLA Modules:
  0.0 266.3 jit_solution(4847820908791265318)
XLA Ops:
  0.6 0.0 copy-start.1
  0.6 236.3 %shard_map.92 = (f32[1024,512]{1,0:T(8,128)}, bf16[8192,512]{1,0:T(8,128)(2,1)}, f32[8,128]{1,0:T(8,128)}) custom-call(bf16[448,8192]{1,0:T(8,128)(2,1)} %pre.1, bf16[448,512]{1,0:T(8,128)(2,1)} %ups.1, bf16[8192,512]{1,0:T(8,128)(2,1)} %w_hbm.1, f32[1024,512]{1,0:T(8,128)} %m.1, f32[1024,512]{1,0:T(8,128)} %v.1), custom_call_target="tpu_custom_call" | custom-call | tf_op jit(solution)/shard_map/pallas_call | solution.py:347
  237.0 1.4 slice_reduce_fusion
  239.7 0.0 copy-done.1
  239.7 0.0 copy-start
  239.8 6.5 %add_multiply_fusion = (f32[1024,512]{1,0:T(8,128)}, f32[1024,512]{1,0:T(8,128)}, f32[1024,512]{1,0:T(8,128)}) fusion(bf16[8192,512]{1,0:T(8,128)(2,1)} %w_hbm.1, s32[]{:T(128)S(6)} %select_n.8, f32[]{:T(128)S(6)} %div.14, f32[1024,512]{1,0:T(8,128)} %get-tuple-element.10, f32[1024,512]{1,0:T(8,128)} %v.1, f32[1024,512]{1,0:T(8,128)S(1)} %copy-done.1), kind=kLoop, calls=%fused_computation.4 | loop fusion | flops 7340032 | bytes 13631496 | tf_op jit(solution)/shard_map/mul | solution.py:406
  246.2 0.0 copy-done
  246.2 0.0 copy-start.2
  246.2 8.4 %subtract_convert_fusion = bf16[8192,512]{1,0:T(8,128)(2,1)} fusion(bf16[8192,512]{1,0:T(8,128)(2,1)} %get-tuple-element.9, bf16[8192,512]{1,0:T(8,128)(2,1)S(1)} %copy-done, f32[]{:T(128)S(6)} %div.14), kind=kLoop, calls=%fused_computation | loop fusion | flops 25165824 | bytes 25165828 | tf_op jit(solution)/shard_map/convert_element_type | solution.py:409
  254.6 0.0 copy-done.2
  254.6 11.6 %select_convert_fusion = bf16[448,8192]{1,0:T(8,128)(2,1)} fusion(bf16[448,8192]{1,0:T(8,128)(2,1)} %pre.1, bf16[448,512]{1,0:T(8,128)(2,1)S(1)} %copy-done.2, bf16[8192,512]{1,0:T(8,128)(2,1)} %w_hbm.1), kind=kOutput, calls=%fused_computation.1 | convolution fusion | flops 3769106432 | bytes 23527424 | tf_op jit(solution)/shard_map/dot_general | solution.py:398
Async XLA Ops:
  0.6 239.1 %copy-start.1 = (f32[1024,512]{1,0:T(8,128)S(1)}, f32[1024,512]{1,0:T(8,128)}, u32[]{:S(2)}) copy-start(f32[1024,512]{1,0:T(8,128)} %m.1) | copy-start | bytes 6291460
  239.7 6.5 %copy-start = (bf16[8192,512]{1,0:T(8,128)(2,1)S(1)}, bf16[8192,512]{1,0:T(8,128)(2,1)}, u32[]{:S(2)}) copy-start(bf16[8192,512]{1,0:T(8,128)(2,1)} %w_hbm.1) | copy-start | bytes 25165828
  246.2 8.4 %copy-start.2 = (bf16[448,512]{1,0:T(8,128)(2,1)S(1)}, bf16[448,512]{1,0:T(8,128)(2,1)}, u32[]{:S(2)}) copy-start(bf16[448,512]{1,0:T(8,128)(2,1)} %ups.1) | copy-start | bytes 1376260

commit v4 on v2

--- a/solution.py
+++ b/solution.py
@@ -39,7 +39,7 @@
     steps = nz * chunks
     partner = 2 * z + 1 - x
     below, above = dp - 2, dp + 2
-    lag = nz + 1
+    lag = nz
 
     flips = []
     bit = 1
@@ -256,7 +256,7 @@
         def _():
             rs_step(t)
 
-        @pl.when((t >= nz) & (t % nz == 1))
+        @pl.when((t >= nz) & (t % nz == 0))
         def _():
             finish(t // nz - 1)
 
@@ -270,7 +270,7 @@
 
         return carry
 
-    lax.fori_loop(0, steps + 2, body, 0)
+    lax.fori_loop(0, steps + 1, body, 0)
 
     width = acc.shape[1] // 128
     local = acc[:, 0:128]
@@ -286,7 +286,7 @@
     nsend[0] = local
     norm_copy(0).start()
     done = 0
-    for t in range(steps + 2, steps + lag + 1):
+    for t in range(steps + 1, steps + lag + 1):
         if t - lag < steps:
             ag_step(t - lag)
         agq_step(t - lag - 1)
@@ -298,7 +298,9 @@
                 if done < len(flips):
                     nsend[done] = local
                     norm_copy(done).start()
-    nrm[...] = local
+    weight_sq = jnp.sum(local[0:1], axis=1, keepdims=True)
+    update_sq = jnp.sum(local[1:2], axis=1, keepdims=True)
+    nrm[...] = jnp.broadcast_to(jnp.sqrt(weight_sq) / jnp.sqrt(update_sq), nrm.shape)
 
     def drain(t, carry):
         c, place = t // nz, t % nz
@@ -328,7 +330,7 @@
 def exchange(nz, nmp, preactivation, upstream, weight, first_moment, second_moment):
     rows, width = first_moment.shape
     part = min(rows, 256)
-    first_rows = part * 5 // 8
+    first_rows = part * 13 // 16
     rest = part - first_rows
     chunks = rows // part
     steps = nz * chunks
@@ -337,7 +339,7 @@
     vmem = pl.BlockSpec(memory_space=pltpu.VMEM)
     anyspec = pl.BlockSpec(memory_space=pl.ANY)
     return pl.pallas_call(
-        functools.partial(kernel, nz, nmp, chunks, first_rows, min(nz + 2, steps)),
+        functools.partial(kernel, nz, nmp, chunks, first_rows, min(nz, steps)),
         out_shape=(
             jax.ShapeDtypeStruct((rows, width), jnp.float32),
             jax.ShapeDtypeStruct(weight.shape, jnp.bfloat16),
@@ -394,7 +396,7 @@
     start_row = lax.axis_index("dp") * owned
     own_weight = lax.dynamic_slice_in_dim(weight, start_row, owned, 0).astype(jnp.float32)
     first_next, second_next, update = moments(gradient, first_moment, second_moment, own_weight)
-    ratio = jnp.sqrt(jnp.sum(norms[0])) / jnp.sqrt(jnp.sum(norms[1]))
+    ratio = norms[0, 0]
     trust_step = ratio * update
     new_weight = (
         weight.astype(jnp.float32) - 0.02 * (ratio * updates.astype(jnp.float32))

time: 231 us -> 227 us (0.983)
  Pallas kernels: 201 us -> 196 us
    pallas_call x1, Pallas kernels: 201 us -> 196 us  [exchange(): pl.pallas_call(functools.partial(kernel, nz, nmp, chunks, first_rows, min...]
where the time goes in v4:
time: 227 us; the launch traced here: 225 us
  Pallas kernels  196 us (86%)
  other arithmetic  15.7 us (7%)
  matrix products  11.7 us (5%)
    pallas_call x1, Pallas kernels, exchange(): pl.pallas_call(functools.partial(kernel, nz, nmp, chunks, first_rows, min...  196 us
    dot_general x1, matrix products, per_device(): lax.dot_general(upstream, weight, (((1,), (1,)), ((), ())), preferred_ele...  11.7 us
    convert_element_type x1, other arithmetic, per_device(): new_weight = (weight.astype(jnp.float32) - 0.02 * (ratio * updates.astype...  9.05 us
    mul x1, other arithmetic, per_device(): trust_step = ratio * update  6.6 us

profile of v4, /device:TPU:0, one launch (start us, length us, event | category | flops | bytes accessed | tf_op | source)
XLA Modules:
  0.0 224.8 jit_solution(5702913888426814110)
XLA Ops:
  0.6 0.0 copy-start.1
  0.6 0.0 copy-start.2
  0.7 195.6 %shard_map.92 = (f32[1024,512]{1,0:T(8,128)}, bf16[8192,512]{1,0:T(8,128)(2,1)}, f32[8,128]{1,0:T(8,128)}) custom-call(bf16[448,8192]{1,0:T(8,128)(2,1)} %pre.1, bf16[448,512]{1,0:T(8,128)(2,1)} %ups.1, bf16[8192,512]{1,0:T(8,128)(2,1)} %w_hbm.1, f32[1024,512]{1,0:T(8,128)} %m.1, f32[1024,512]{1,0:T(8,128)} %v.1), custom_call_target="tpu_custom_call" | custom-call | tf_op jit(solution)/shard_map/pallas_call | solution.py:341
  196.3 1.2 slice.3
  197.5 0.0 copy-done.1
  197.5 0.0 copy-done.2
  197.5 0.0 copy-start
  197.5 6.6 %add_multiply_fusion = (f32[1024,512]{1,0:T(8,128)}, f32[1024,512]{1,0:T(8,128)}, f32[1024,512]{1,0:T(8,128)}) fusion(bf16[8192,512]{1,0:T(8,128)(2,1)} %w_hbm.1, s32[]{:T(128)S(6)} %select_n.8, f32[]{:T(128)} %bitcast, f32[1024,512]{1,0:T(8,128)} %get-tuple-element.10, f32[1024,512]{1,0:T(8,128)S(1)} %copy-done.2, f32[1024,512]{1,0:T(8,128)S(1)} %copy-done.1), kind=kLoop, calls=%fused_computation.4 | loop fusion | flops 7340032 | bytes 13631496 | tf_op jit(solution)/shard_map/mul | solution.py:400
  204.1 0.0 copy-done
  204.1 0.0 copy-start.3
  204.1 9.1 %subtract_convert_fusion = bf16[8192,512]{1,0:T(8,128)(2,1)} fusion(bf16[8192,512]{1,0:T(8,128)(2,1)} %get-tuple-element.9, bf16[8192,512]{1,0:T(8,128)(2,1)S(1)} %copy-done, f32[]{:T(128)} %bitcast), kind=kLoop, calls=%fused_computation | loop fusion | flops 25165824 | bytes 25165828 | tf_op jit(solution)/shard_map/convert_element_type | solution.py:403
  213.1 0.0 copy-done.3
  213.1 11.7 %select_convert_fusion = bf16[448,8192]{1,0:T(8,128)(2,1)} fusion(bf16[448,8192]{1,0:T(8,128)(2,1)} %pre.1, bf16[448,512]{1,0:T(8,128)(2,1)S(1)} %copy-done.3, bf16[8192,512]{1,0:T(8,128)(2,1)} %w_hbm.1), kind=kOutput, calls=%fused_computation.1 | convolution fusion | flops 3769106432 | bytes 23527424 | tf_op jit(solution)/shard_map/dot_general | solution.py:392
Async XLA Ops:
  0.6 196.8 %copy-start.1 = (f32[1024,512]{1,0:T(8,128)S(1)}, f32[1024,512]{1,0:T(8,128)}, u32[]{:S(2)}) copy-start(f32[1024,512]{1,0:T(8,128)} %m.1) | copy-start | bytes 6291460
  0.6 196.8 %copy-start.2 = (f32[1024,512]{1,0:T(8,128)S(1)}, f32[1024,512]{1,0:T(8,128)}, u32[]{:S(2)}) copy-start(f32[1024,512]{1,0:T(8,128)} %v.1) | copy-start | bytes 6291460
  197.5 6.6 %copy-start = (bf16[8192,512]{1,0:T(8,128)(2,1)S(1)}, bf16[8192,512]{1,0:T(8,128)(2,1)}, u32[]{:S(2)}) copy-start(bf16[8192,512]{1,0:T(8,128)(2,1)} %w_hbm.1) | copy-start | bytes 25165828
  204.1 9.1 %copy-start.3 = (bf16[448,512]{1,0:T(8,128)(2,1)S(1)}, bf16[448,512]{1,0:T(8,128)(2,1)}, u32[]{:S(2)}) copy-start(bf16[448,512]{1,0:T(8,128)(2,1)} %ups.1) | copy-start | bytes 1376260
